TPU v7x, 32 devices: a whole 2x2x4 slice. The times are simulated.
32 devices in a mesh: groups: 2 (over y), tile: 4 (over z), segment: 2 (over core), mp: 2 (over x).
Axes of the slice: x: 2, y: 2, z: 4, core: 2. Of those that a mesh axis runs over, the one named last changes fastest.
Arguments:
- spectra: bfloat16 [2, 64, 48, 224], P(None, ('groups', 'tile')), parts along dimension 1, may hold values from -6 to 6
- valid: int32 [2, 64], P(None, 'groups'), parts along dimension 1, may hold values from 1 to 48, as said below
- project: bfloat16 [224, 16], replicated, may hold values from -0.375 to 0.375
- enc_in: bfloat16 [768, 3072], P(None, 'mp'), may hold values from -0.21875 to 0.21875
- enc_out: bfloat16 [3072, 768], P('mp'), may hold values from -0.109375 to 0.109375
- tok_embed: bfloat16 [48, 2048], replicated, may hold values from -0.875 to 0.875
- band_embed: bfloat16 [16, 2048], P('tile'), may hold values from -3 to 3
- dec_in: bfloat16 [2048, 8192], P('tile', 'mp'), may hold values from -0.125 to 0.125
- dec_out: bfloat16 [8192, 2048], P('mp', 'tile'), may hold values from -0.0625 to 0.0625
- head: bfloat16 [2048, 672], P('tile', 'mp'), may hold values from -0.125 to 0.125
Outputs:
- grad_project: float32 [448, 16], P(('groups', 'tile', 'segment')), parts along dimension 0
- grad_enc_in: float32 [1536, 3072], P(('groups', 'tile', 'segment'), 'mp'), parts along dimension 0
- grad_enc_out: float32 [6144, 768], P(('groups', 'mp'), ('tile', 'segment')), parts along dimension 0
There are 2 independent parts, one for each index of `groups`. A program takes and returns all parts, laid end to end along the dimension named above; an argument that names none is the same for every part. Nothing has to cross between parts.
Inputs may be any that keep to these rules, and one draw needn't show every extreme that they name: Pixels of patch n in micro-batch m with index below valid[m, n] count in the loss.
All inputs are finite; a program needn't handle non-finite values.
Results may differ from a plain program's by a relative error of at most 0.018.
Values may be sent and summed in bfloat16 or wider, within the bound.
A program may use at most 128 MiB of HBM per device.

v0:
```python
import jax
import jax.numpy as jnp
from jax import lax
from jax.sharding import PartitionSpec as P

BF = jnp.bfloat16
F32 = jnp.float32


def inv_rms(values):
    return lax.rsqrt(jnp.mean(values * values, axis=-1, keepdims=True) + 1e-05)


def rms_back(values, gradient):
    scaling = inv_rms(values)
    normed = values * scaling
    return scaling * (gradient - normed * jnp.mean(gradient * normed, axis=-1, keepdims=True))


def gelu(v):
    return 0.5 * v * (1 + jnp.tanh(0.7978845608028654 * (v + 0.044715 * v * v * v)))


def gelu_and_slope(v):
    square = v * v
    t = jnp.tanh(0.7978845608028654 * v * (1 + 0.044715 * square))
    half = 0.5 * (1 + t)
    slope = half + 0.5 * v * (1 - t * t) * 0.7978845608028654 * (1 + 3 * 0.044715 * square)
    return (v * half, slope)


def dot(a, b):
    return jnp.dot(a, b, preferred_element_type=F32)


def dot_t(a, b):
    return lax.dot_general(a, b, (((1,), (1,)), ((), ())), preferred_element_type=F32)


def t_dot(a, b):
    return lax.dot_general(a, b, (((0,), (0,)), ((), ())), preferred_element_type=F32)


def body(spectra, valid, project, enc_in, enc_out, tok_embed, band_embed, dec_in, dec_out, head):
    tile, seg, mp = (lax.axis_index(a) for a in ("tile", "segment", "mp"))
    T, S, M = (lax.axis_size(a) for a in ("tile", "segment", "mp"))
    batches, per_tile, pixels, bands = spectra.shape
    codes = project.shape[1]
    width = bands // codes
    local = batches * per_tile
    share = local // (S * M)
    rows = T * local
    student = codes * pixels
    dim = tok_embed.shape[1]
    dt = dec_in.shape[0]
    hid = dec_in.shape[1] // S
    once = jnp.logical_and(seg == 0, mp == 0).astype(F32)
    patches = spectra.reshape(local, pixels, bands)
    flat = patches.reshape(local * pixels, bands)
    feat_local = (
        dot(flat, project)
        .astype(BF)
        .reshape(local, pixels, codes)
        .transpose(0, 2, 1)
        .reshape(local, student)
    )
    feats = lax.all_gather(feat_local, "tile")
    feats = feats.reshape(T, S, M, share, student).transpose(1, 2, 0, 3, 4).reshape(rows, student)
    band_all = lax.all_gather(band_embed, "tile", tiled=True)
    head_full = lax.all_gather(head, "mp", axis=1, tiled=True)
    embed = jnp.concatenate([tok_embed, band_all], axis=0)
    embed_z = lax.dynamic_slice_in_dim(embed, tile * dt, dt, 1)
    d_in = lax.dynamic_slice_in_dim(dec_in, seg * hid, hid, 1)
    d_out = lax.dynamic_slice_in_dim(dec_out, seg * hid, hid, 0)
    folded = lax.psum(dot(embed_z, d_in).astype(BF), "tile")
    fold_tok, fold_band = (folded[:pixels], folded[pixels:])
    feats32 = feats.astype(F32)
    normed = (feats32 * inv_rms(feats32)).astype(BF)
    pre_act, pre_slope = gelu_and_slope(dot(normed, enc_in))
    act_out = pre_act.astype(BF)
    summed = lax.psum(dot(act_out, enc_out).astype(BF), "mp").astype(F32)
    encoded = (feats32 + summed).astype(BF)
    tokens = rows * codes
    tok = encoded.reshape(tokens, pixels)
    embedded = (
        (dot(tok, tok_embed).reshape(rows, codes, dim) + band_all.astype(F32))
        .reshape(tokens, dim)
        .astype(BF)
    )
    scaling = inv_rms(embedded.astype(F32))
    hid_pre = scaling * (
        dot(tok, fold_tok).reshape(rows, codes, hid) + fold_band.astype(F32)
    ).reshape(tokens, hid)
    hid_act, hid_slope = gelu_and_slope(hid_pre)
    embedded_z = lax.dynamic_slice_in_dim(embedded, tile * dt, dt, 1)
    decoded = (once * embedded_z.astype(F32) + dot(hid_act.astype(BF), d_out)).astype(BF)
    partial = dot(decoded, head_full).astype(BF)
    own = lax.psum_scatter(
        partial.reshape(S * M, T, share * codes, -1), ("segment", "mp"), scatter_dimension=0
    )
    own = lax.psum_scatter(own, "tile", scatter_dimension=0).astype(F32)
    quarter = (seg * M + mp) * share
    own_patches = lax.dynamic_slice_in_dim(patches, quarter, share, 0)
    target = (
        own_patches.reshape(share, pixels, codes, width)
        .transpose(0, 2, 1, 3)
        .reshape(share * codes, -1)
    )
    total_valid = jnp.sum(valid.astype(F32))
    loss_scale = 2.0 * batches * valid.shape[1] / total_valid
    own_valid = lax.dynamic_slice_in_dim(valid, tile * per_tile, per_tile, 1).reshape(local)
    own_valid = lax.dynamic_slice_in_dim(own_valid, quarter, share, 0)
    column = jnp.arange(pixels * width, dtype=jnp.int32) // width
    mask = (column[None, :] < jnp.repeat(own_valid, codes)[:, None]).astype(F32)
    grad_own = (loss_scale * mask * (own - target.astype(F32))).astype(BF)
    grad_rebuilt = lax.all_gather(lax.all_gather(grad_own, "tile"), ("segment", "mp")).reshape(
        tokens, -1
    )
    grad_decoded = dot_t(grad_rebuilt, head_full).astype(BF)
    grad_hid = hid_slope * dot_t(grad_decoded, d_out)
    tok_z = lax.dynamic_slice_in_dim(tok_embed, tile * dt, dt, 1)
    unit_tok = dot_t((embedded.astype(F32) * scaling).astype(BF), tok_embed)
    along = jnp.sum(grad_hid * hid_pre, axis=1, keepdims=True) / dim
    grad_tok = scaling * (dot_t(grad_hid.astype(BF), fold_tok) - unit_tok * along)
    grad_tok = grad_tok + once * dot_t(grad_decoded, tok_z)
    grad_encoded = lax.psum(grad_tok.reshape(rows, student).astype(BF), ("tile", "segment", "mp"))
    grad_act = (pre_slope * dot_t(grad_encoded, enc_out)).astype(BF)
    columns = student // (T * S)
    start = (tile * S + seg) * columns
    grad_out = t_dot(act_out, lax.dynamic_slice_in_dim(grad_encoded, start, columns, 1))
    grad_in = t_dot(lax.dynamic_slice_in_dim(normed, start, columns, 1), grad_act)
    grad_normed = lax.psum(dot_t(grad_act, enc_in).astype(BF), "mp").astype(F32)
    own_rows = lambda a: lax.dynamic_slice_in_dim(
        a.reshape(S * M, T, share, student), tile, 1, 1
    ).reshape(local, student)
    grad_feat = (
        own_rows(grad_encoded).astype(F32) + rms_back(feat_local.astype(F32), own_rows(grad_normed))
    ).astype(BF)
    grad_codes = grad_feat.reshape(local, codes, pixels).transpose(0, 2, 1).reshape(-1, codes)
    grad_proj = jnp.sum(lax.all_gather(t_dot(flat, grad_codes), "tile"), axis=0)
    proj_rows = bands // (T * S)
    grad_proj = lax.dynamic_slice_in_dim(grad_proj, (tile * S + seg) * proj_rows, proj_rows, 0)
    return (grad_proj, grad_in, grad_out)


def solution(mesh):
    placed = (
        P(None, ("groups", "tile"), None, None),
        P(None, "groups"),
        P(),
        P(None, "mp"),
        P("mp", None),
        P(),
        P("tile", None),
        P("tile", "mp"),
        P("mp", "tile"),
        P("tile", "mp"),
    )
    return jax.shard_map(
        body,
        mesh=mesh,
        in_specs=placed,
        out_specs=(
            P(("groups", "tile", "segment"), None),
            P(("groups", "tile", "segment"), "mp"),
            P(("groups", "mp"), ("tile", "segment")),
        ),
        check_vma=False,
    )
```

profile of v0, /device:TPU:0, one launch (start us, length us, event | category | flops | bytes accessed | tf_op | source)
XLA Modules:
  0.0 350.5 jit_solution(10092934858017082224)
XLA Ops:
  9.6 15.0 %all_gather.25 = bf16[4,16,768]{2,1,0:T(8,128)(2,1)S(1)} all-gather(bf16[1,16,768]{2,1,0:T(8,128)(2,1)S(1)} %all_gather_reshape.3), channel_id=1, replica_groups=mesh['groups'=2,'tile'=4,'segment'=2,'mp'=2] {'tile'}, dimensions={0}, use_global_device_ids=true | all-gather | bytes 122880 | tf_op jit(solution)/shard_map/all_gather | solution.py:67
  25.2 2.2 fusion.50
  29.5 13.3 %all-gather.2 = bf16[4,4,2048]{2,1,0:T(4,128)(2,1)S(1)} all-gather(bf16[1,4,2048]{2,1,0:T(4,128)(2,1)S(1)} %bitcast.88), channel_id=1, replica_groups=mesh['groups'=2,'tile'=4,'segment'=2,'mp'=2] {'tile'}, dimensions={0}, use_global_device_ids=true | all-gather | bytes 81920 | tf_op jit(solution)/shard_map/all_gather | solution.py:69
  42.8 2.8 convolution_convert_fusion
  46.4 8.4 %all_gather.27 = bf16[512,672]{0,1:T(8,128)(2,1)S(1)} all-gather(bf16[512,336]{0,1:T(8,128)(2,1)} %param.19), channel_id=1, replica_groups=mesh['groups'=2,'tile'=4,'segment'=2,'mp'=2] {'mp'}, dimensions={1}, use_global_device_ids=true | all-gather | bytes 1032192 | tf_op jit(solution)/shard_map/all_gather | solution.py:70
  56.1 4.2 %multiply_reduce_fusion.1 = (f32[64,16]{1,0:T(8,128)S(1)}, bf16[64,16,2048]{2,1,0:T(8,128)(2,1)}) fusion(f32[16,2048]{1,0:T(8,128)} %convert_element_type.165, bf16[64,16,48]{2,1,0:T(8,128)(2,1)S(1)} %dot_general.61, bf16[48,2048]{1,0:T(8,128)(2,1)} %param.15), kind=kOutput, calls=%fused_computation.7 | convolution fusion | flops 211811328 | bytes 4624384 | tf_op jit(solution)/shard_map/dot_general | solution.py:33
  60.4 29.6 %all-reduce.7.cloned.1.call-done = bf16[64,2048]{1,0:T(8,128)(2,1)} async-done(((bf16[64,2048]{1,0:T(8,128)(2,1)}), bf16[64,2048]{1,0:T(8,128)(2,1)}) %all-reduce.7.cloned.1.call-update) | async-done | bytes 262160 | tf_op jit(solution)/shard_map/psum | solution.py:75
  90.8 2.2 convolution_add_fusion
  93.0 5.3 %multiply_convert_fusion.1 = bf16[1024,2048]{1,0:T(8,128)(2,1)} fusion(f32[64,16,2048]{2,1,0:T(8,128)S(1)} %convolution_add_fusion, f32[1024]{0:T(1024)S(1)} %rsqrt.37), kind=kLoop, calls=%fused_computation.3 | loop fusion | flops 20971520 | bytes 12587008 | tf_op jit(solution)/shard_map/convert_element_type | solution.py:96
  98.3 7.2 %convolution_convert_fusion.1 = bf16[1024,672]{0,1:T(8,128)(2,1)} fusion(bf16[512,672]{0,1:T(8,128)(2,1)S(1)} %all_gather.27, bf16[1024,2048]{1,0:T(8,128)(2,1)} %multiply_convert_fusion.1, bf16[4096,512]{1,0:T(8,128)(2,1)} %param.18, s32[]{:T(128)S(6)} %select_n.37, bf16[1024,2048]{1,0:T(8,128)(2,1)} %bitcast.90, s32[]{:T(128)S(6)} %select_n.36, ...), kind=kOutput, calls=%fused_computation.22 | convolution fusion | flops 2854912000 | bytes 9404428 | tf_op jit(solution)/shard_map/dot_general | solution.py:33
  105.5 2.6 copy.40
  108.2 28.0 %reduce-scatter.3.cloned.1.call-done = bf16[1,4,64,672]{3,2,1,0:T(8,128)(2,1)} async-done(((bf16[4,4,64,672]{3,2,1,0:T(8,128)(2,1)}), bf16[1,4,64,672]{3,2,1,0:T(8,128)(2,1)}) %reduce-scatter.3.cloned.1.call-update) | async-done | bytes 344080 | tf_op jit(solution)/shard_map/reduce_scatter | solution.py:98
  138.7 1.9 reshape.268
  142.0 17.0 %reduce-scatter.5.cloned.1.call-done = bf16[1,64,672]{2,1,0:T(8,128)(2,1)} async-done(((bf16[4,64,672]{2,1,0:T(8,128)(2,1)}), bf16[1,64,672]{2,1,0:T(8,128)(2,1)}) %reduce-scatter.5.cloned.1.call-update) | async-done | bytes 86032 | tf_op jit(solution)/shard_map/reduce_scatter | solution.py:101
  160.0 15.8 %all_gather.28 = bf16[4,64,672]{2,1,0:T(8,128)(2,1)} all-gather(bf16[1,64,672]{2,1,0:T(8,128)(2,1)S(1)} %multiply_convert_fusion.6), channel_id=1, replica_groups=mesh['groups'=2,'tile'=4,'segment'=2,'mp'=2] {'tile'}, dimensions={0}, use_global_device_ids=true | all-gather | bytes 430080 | tf_op jit(solution)/shard_map/all_gather | solution.py:116
  176.2 17.2 %all-gather.6.cloned.1.call-done = bf16[16,64,672]{2,1,0:T(8,128)(2,1)} async-done(((bf16[4,64,672]{2,1,0:T(8,128)(2,1)}), bf16[16,64,672]{2,1,0:T(8,128)(2,1)}) %all-gather.6.cloned.1.call-update) | async-done | bytes 1376272 | tf_op jit(solution)/shard_map/all_gather | solution.py:116
  193.4 2.7 convolution_convert_fusion.2
  196.3 9.2 %multiply_reduce_fusion = (f32[1024]{0:T(1024)S(1)}, bf16[1024,2048]{1,0:T(8,128)(2,1)S(1)}) fusion(f32[64,16,2048]{2,1,0:T(8,128)} %copy-done.1, f32[1024]{0:T(1024)S(1)} %rsqrt.37, bf16[1024,512]{1,0:T(8,128)(2,1)S(1)} %convolution_convert_fusion.2, bf16[4096,512]{1,0:T(8,128)(2,1)S(1)} %copy-done.12, s32[]{:T(128)S(6)} %select_n.37), kind=kOutput, calls=%fused_computation.1 | convolution fusion | flops 2191522816 | bytes 15736836 | tf_op jit(solution)/shard_map/dot_general | solution.py:37
  207.5 2.0 fusion.21
  212.7 86.1 %all-reduce.9.cloned.1.call-done = bf16[64,768]{1,0:T(8,128)(2,1)} async-done(((bf16[64,768]{1,0:T(8,128)(2,1)}), bf16[64,768]{1,0:T(8,128)(2,1)}) %all-reduce.9.cloned.1.call-update) | async-done | bytes 98320 | tf_op jit(solution)/shard_map/psum | solution.py:126
  300.5 3.1 convolution_convert_fusion.3
  307.2 1.9 fusion.34
  310.2 17.2 %all-reduce.11.cloned.1.call-done = bf16[4,4,4,768]{3,2,0,1:T(4,128)(2,1)} async-done(((bf16[4,4,4,768]{3,2,0,1:T(4,128)(2,1)}), bf16[4,4,4,768]{3,2,0,1:T(4,128)(2,1)}) %all-reduce.11.cloned.1.call-update) | async-done | bytes 98320 | tf_op jit(solution)/shard_map/psum | solution.py:132
  329.7 13.3 %all-gather.3 = f32[4,224,16]{1,2,0:T(8,128)S(1)} all-gather(f32[1,224,16]{1,2,0:T(8,128)S(1)} %convolution_bitcast_fusion), channel_id=3, replica_groups=mesh['groups'=2,'tile'=4,'segment'=2,'mp'=2] {'tile'}, dimensions={0}, use_global_device_ids=true | all-gather | bytes 71680 | tf_op jit(solution)/shard_map/all_gather | solution.py:140
  (102 shorter events, 26.9 us)
Async XLA Ops:
  7.2 21.0 %copy-start = (bf16[1536,768]{1,0:T(8,128)(2,1)S(1)}, bf16[1536,768]{1,0:T(8,128)(2,1)}, u32[]{:S(2)}) copy-start(bf16[1536,768]{1,0:T(8,128)(2,1)} %param.14) | copy-start | bytes 7077892
  7.2 22.3 %copy-start.10 = (bf16[4,2048]{1,0:T(4,128)(2,1)S(1)}, bf16[4,2048]{1,0:T(4,128)(2,1)}, u32[]{:S(2)}) copy-start(bf16[4,2048]{1,0:T(4,128)(2,1)} %param.16) | copy-start | bytes 49156
  7.2 47.6 %all-reduce.5.cloned.1.call-start = ((), (), s32[]{:S(2)}) async-start(), calls=%async_computation.2 | async-start | bytes 196608 | tf_op jit(solution)/shard_map/psum | solution.py:81
  7.2 35.6 %copy-start.8 = (bf16[48,2048]{1,0:T(8,128)(2,1)S(1)}, bf16[48,2048]{1,0:T(8,128)(2,1)}, u32[]{:S(2)}) copy-start(bf16[48,2048]{1,0:T(8,128)(2,1)} %param.15) | copy-start | bytes 589828
  25.2 4.3 %copy-start.7 = (bf16[64,768]{1,0:T(8,128)(2,1)}, bf16[64,768]{1,0:T(8,128)(2,1)S(1)}, u32[]{:S(2)}) copy-start(bf16[64,768]{1,0:T(8,128)(2,1)S(1)} %multiply_convert_fusion.7) | copy-start | bytes 294916
  27.4 0.8 copy-start.3
  29.4 60.6 %all-reduce.7.cloned.1.call-start = ((), (), s32[]{:S(2)}) async-start(), calls=%async_computation.3 | async-start | bytes 524288 | tf_op jit(solution)/shard_map/psum | solution.py:75
  45.6 90.6 %reduce-scatter.3.cloned.1.call-start = ((), (), s32[]{:S(2)}) async-start(), calls=%async_computation.4 | async-start | bytes 1966080 | tf_op jit(solution)/shard_map/reduce_scatter | solution.py:98
  54.7 43.5 %copy-start.6 = (bf16[512,672]{0,1:T(8,128)(2,1)}, bf16[512,672]{0,1:T(8,128)(2,1)S(1)}, u32[]{:S(2)}) copy-start(bf16[512,672]{0,1:T(8,128)(2,1)S(1)} %all_gather.27) | copy-start | bytes 2064388
  93.0 5.3 %copy-start.1 = (f32[64,16,2048]{2,1,0:T(8,128)}, f32[64,16,2048]{2,1,0:T(8,128)S(1)}, u32[]{:S(2)}) copy-start(f32[64,16,2048]{2,1,0:T(8,128)S(1)} %convolution_add_fusion) | copy-start | bytes 25165828
  105.5 30.8 %copy-start.11 = (s32[2,32]{1,0:T(2,128)S(1)}, s32[2,32]{1,0:T(2,128)}, u32[]{:S(2)}) copy-start(s32[2,32]{1,0:T(2,128)} %param.11) | copy-start | bytes 772
  105.5 31.2 %copy-start.2 = (bf16[2,8,48,224]{3,2,1,0:T(8,128)(2,1)S(1)}, bf16[2,8,48,224]{3,2,1,0:T(8,128)(2,1)}, u32[]{:S(2)}) copy-start(bf16[2,8,48,224]{3,2,1,0:T(8,128)(2,1)} %param.10) | copy-start | bytes 1032196
  108.1 50.8 %reduce-scatter.5.cloned.1.call-start = ((), (), s32[]{:S(2)}) async-start(), calls=%async_computation.5 | async-start | bytes 491520 | tf_op jit(solution)/shard_map/reduce_scatter | solution.py:101
  136.2 57.2 %all-gather.6.cloned.1.call-start = ((), (), s32[]{:S(2)}) async-start(), calls=%async_computation.8 | async-start | bytes 1966080 | tf_op jit(solution)/shard_map/all_gather | solution.py:116
  175.8 123.0 %all-reduce.9.cloned.1.call-start = ((), (), s32[]{:S(2)}) async-start(), calls=%async_computation.6 | async-start | bytes 196608 | tf_op jit(solution)/shard_map/psum | solution.py:126
  193.4 2.9 copy-start.12
  196.3 9.2 %copy-start.9 = (bf16[48,2048]{1,0:T(8,128)(2,1)S(1)}, bf16[48,2048]{1,0:T(8,128)(2,1)}, u32[]{:S(2)}) copy-start(bf16[48,2048]{1,0:T(8,128)(2,1)} %param.15) | copy-start | bytes 589828
  196.3 9.7 %copy-start.13 = (bf16[64,16,2048]{2,1,0:T(8,128)(2,1)S(1)}, bf16[64,16,2048]{2,1,0:T(8,128)(2,1)}, u32[]{:S(2)}) copy-start(bf16[64,16,2048]{2,1,0:T(8,128)(2,1)} %get-tuple-element.6) | copy-start | bytes 12582916
  206.0 1.5 copy-start.5
  207.5 91.4 %copy-start.4 = (f32[64,1536]{1,0:T(8,128)S(1)}, f32[64,1536]{1,0:T(8,128)}, u32[]{:S(2)}) copy-start(f32[64,1536]{1,0:T(8,128)} %copy-done.3) | copy-start | bytes 1179652
  211.5 115.9 %all-reduce.11.cloned.1.call-start = ((), (), s32[]{:S(2)}) async-start(), calls=%async_computation.7 | async-start | bytes 196608 | tf_op jit(solution)/shard_map/psum | solution.py:132
Sparse Core Ops, SparseCore 0:
  29.5 22.1 all-reduce.4
  54.6 35.3 all-reduce.6
  108.3 27.9 reduce-scatter.2
  138.3 20.5 reduce-scatter.4
  175.9 17.4 all-gather.5
  211.6 87.1 all-reduce.8
  307.3 20.0 all-reduce.10
where the time goes:
time: 351 us; the launch traced here: 350 us
  waiting for transfers between devices  195 us (56%)
  blocking collectives  65.8 us (19%)
  matrix products  45.8 us (13%)
  local copies, waits for them, and re-layouts  15.7 us (4%)
  between operations  15.2 us (4%)
  other arithmetic  12.3 us (4%)
    psum x1, waiting for transfers between devices, body(): lax.psum(grad_tok.reshape(rows, student).astype(BF), ('tile', 'segment',...  86.1 us
    psum x1, waiting for transfers between devices, body(): folded = lax.psum(dot(embed_z, d_in).astype(BF), 'tile')  29.6 us
    reduce_scatter x1, waiting for transfers between devices, body(): lax.psum_scatter(partial.reshape(S * M, T, share * codes, -1), ('segment'...  28 us
    dot_general x7, matrix products, dot(): return jnp.dot(a, b, preferred_element_type=F32)  21.1 us
    dot_general x7, matrix products, dot_t(): lax.dot_general(a, b, (((1,), (1,)), ((), ())), preferred_element_type=F32)  20.7 us
    all_gather x1, waiting for transfers between devices, body(): lax.all_gather(lax.all_gather(grad_own, 'tile'), ('segment', 'mp'))  17.2 us
    psum x1, waiting for transfers between devices, body(): grad_normed = lax.psum(dot_t(grad_act, enc_in).astype(BF), 'mp').astype(F32)  17.2 us
    reduce_scatter x1, waiting for transfers between devices, body(): own = lax.psum_scatter(own, 'tile', scatter_dimension=0).astype(F32)  17 us
  transfers between devices with their start and end apart: 7, of which 6 were waited for; matrix products, arithmetic and copies ran while one was open for 5% of the time, Pallas kernels for 0%

commit v1 on v0

--- a/solution.py
+++ b/solution.py
@@ -5,6 +5,18 @@
 
 BF = jnp.bfloat16
 F32 = jnp.float32
+
+
+def collect(x, axis, dim):
+    ways, here, lap = (lax.axis_size(axis), lax.axis_index(axis), x.shape[dim])
+    line, have = (x, 1)
+    while have < ways:
+        line = jnp.concatenate(
+            [line, lax.ppermute(line, axis, [(d, (d - have) % ways) for d in range(ways)])],
+            axis=dim,
+        )
+        have = 2 * have
+    return jnp.roll(line, here * lap, axis=dim)
 
 
 def inv_rms(values):
@@ -67,7 +79,7 @@
     feats = lax.all_gather(feat_local, "tile")
     feats = feats.reshape(T, S, M, share, student).transpose(1, 2, 0, 3, 4).reshape(rows, student)
     band_all = lax.all_gather(band_embed, "tile", tiled=True)
-    head_full = lax.all_gather(head, "mp", axis=1, tiled=True)
+    head_full = collect(head, "mp", 1)
     embed = jnp.concatenate([tok_embed, band_all], axis=0)
     embed_z = lax.dynamic_slice_in_dim(embed, tile * dt, dt, 1)
     d_in = lax.dynamic_slice_in_dim(dec_in, seg * hid, hid, 1)

time: 351 us -> 355 us (1.011)
  blocking collectives: 65.8 us -> 57.3 us
  waiting for transfers between devices: 195 us -> 202 us
    all_gather x1 -> x0, blocking collectives: 8.39 us -> none  [body(): head_full = lax.all_gather(head, 'mp', axis=1, tiled=True)]
    psum x1, waiting for transfers between devices: 0.01 us -> 3.98 us  [body(): summed = lax.psum(dot(act_out, enc_out).astype(BF), 'mp').astype(F32)]
  transfers between devices with their start and end apart: 7 -> 8, of which waited for: 6 -> 7; matrix products, arithmetic and copies ran while one was open for 5% -> 7% of each run, Pallas kernels for 0% -> 0%
where the time goes in v1:
time: 355 us; the launch traced here: 354 us
  waiting for transfers between devices  202 us (57%)
  blocking collectives  57.3 us (16%)
  matrix products  45.7 us (13%)
  local copies, waits for them, and re-layouts  16.6 us (5%)
  between operations  15.2 us (4%)
  other arithmetic  14.8 us (4%)
    psum x1, waiting for transfers between devices, body(): lax.psum(grad_tok.reshape(rows, student).astype(BF), ('tile', 'segment',...  86.1 us
    psum x1, waiting for transfers between devices, body(): folded = lax.psum(dot(embed_z, d_in).astype(BF), 'tile')  32.9 us
    reduce_scatter x1, waiting for transfers between devices, body(): lax.psum_scatter(partial.reshape(S * M, T, share * codes, -1), ('segment'...  28.1 us
    dot_general x7, matrix products, dot(): return jnp.dot(a, b, preferred_element_type=F32)  21 us
    dot_general x7, matrix products, dot_t(): lax.dot_general(a, b, (((1,), (1,)), ((), ())), preferred_element_type=F32)  20.7 us
    all_gather x1, waiting for transfers between devices, body(): lax.all_gather(lax.all_gather(grad_own, 'tile'), ('segment', 'mp'))  17.4 us
    psum x1, waiting for transfers between devices, body(): grad_normed = lax.psum(dot_t(grad_act, enc_in).astype(BF), 'mp').astype(F32)  17.2 us
    reduce_scatter x1, waiting for transfers between devices, body(): own = lax.psum_scatter(own, 'tile', scatter_dimension=0).astype(F32)  16.8 us
  transfers between devices with their start and end apart: 8, of which 7 were waited for; matrix products, arithmetic and copies ran while one was open for 7% of the time, Pallas kernels for 0%

profile of v1, /device:TPU:0, one launch (start us, length us, event | category | flops | bytes accessed | tf_op | source)
XLA Modules:
  0.0 353.9 jit_solution(9914980210259476359)
XLA Ops:
  9.6 15.0 %all_gather.22 = bf16[4,16,768]{2,1,0:T(8,128)(2,1)S(1)} all-gather(bf16[1,16,768]{2,1,0:T(8,128)(2,1)S(1)} %all_gather_reshape.3), channel_id=1, replica_groups=mesh['groups'=2,'tile'=4,'segment'=2,'mp'=2] {'tile'}, dimensions={0}, use_global_device_ids=true | all-gather | bytes 122880 | tf_op jit(solution)/shard_map/all_gather | solution.py:79
  25.2 2.2 fusion.53
  31.0 13.1 %all-gather.2 = bf16[4,4,2048]{2,1,0:T(4,128)(2,1)S(1)} all-gather(bf16[1,4,2048]{2,1,0:T(4,128)(2,1)S(1)} %bitcast.88), channel_id=1, replica_groups=mesh['groups'=2,'tile'=4,'segment'=2,'mp'=2] {'tile'}, dimensions={0}, use_global_device_ids=true | all-gather | bytes 81920 | tf_op jit(solution)/shard_map/all_gather | solution.py:81
  44.2 2.8 convolution_convert_fusion
  47.7 4.0 %all-reduce.5.cloned.1.call-done = bf16[64,768]{1,0:T(8,128)(2,1)} async-done(((bf16[64,768]{1,0:T(8,128)(2,1)}), bf16[64,768]{1,0:T(8,128)(2,1)}) %all-reduce.5.cloned.1.call-update) | async-done | bytes 98320 | tf_op jit(solution)/shard_map/psum | solution.py:93
  52.9 4.1 %multiply_reduce_fusion.1 = (f32[64,16]{1,0:T(8,128)S(1)}, bf16[64,16,2048]{2,1,0:T(8,128)(2,1)}) fusion(f32[16,2048]{1,0:T(8,128)} %convert_element_type.165, bf16[64,16,48]{2,1,0:T(8,128)(2,1)S(1)} %dot_general.61, bf16[48,2048]{1,0:T(8,128)(2,1)S(1)} %copy-done.9), kind=kOutput, calls=%fused_computation.7 | convolution fusion | flops 211811328 | bytes 4624384 | tf_op jit(solution)/shard_map/dot_general | solution.py:45
  57.1 32.9 %all-reduce.7.cloned.1.call-done = bf16[64,2048]{1,0:T(8,128)(2,1)} async-done(((bf16[64,2048]{1,0:T(8,128)(2,1)}), bf16[64,2048]{1,0:T(8,128)(2,1)}) %all-reduce.7.cloned.1.call-update) | async-done | bytes 262160 | tf_op jit(solution)/shard_map/psum | solution.py:87
  90.8 2.2 convolution_add_fusion
  93.0 5.3 %multiply_convert_fusion.1 = bf16[1024,2048]{1,0:T(8,128)(2,1)} fusion(f32[64,16,2048]{2,1,0:T(8,128)S(1)} %convolution_add_fusion, f32[1024]{0:T(1024)S(1)} %rsqrt.37), kind=kLoop, calls=%fused_computation.3 | loop fusion | flops 20971520 | bytes 12587008 | tf_op jit(solution)/shard_map/convert_element_type | solution.py:108
  98.3 2.6 fusion.28
  101.8 7.2 %convolution_convert_fusion.1 = bf16[1024,672]{0,1:T(8,128)(2,1)} fusion(bf16[512,672]{0,1:T(8,128)(2,1)S(1)} %fusion.28, bf16[1024,2048]{1,0:T(8,128)(2,1)} %multiply_convert_fusion.1, bf16[4096,512]{1,0:T(8,128)(2,1)} %param.18, s32[]{:T(128)S(6)} %select_n.50, bf16[1024,2048]{1,0:T(8,128)(2,1)} %bitcast.90, s32[]{:T(128)S(6)} %select_n.49, ...), kind=kOutput, calls=%fused_computation.22 | convolution fusion | flops 2854912000 | bytes 9404428 | tf_op jit(solution)/shard_map/dot_general | solution.py:45
  109.0 2.6 copy.40
  111.7 28.1 %reduce-scatter.3.cloned.1.call-done = bf16[1,4,64,672]{3,2,1,0:T(8,128)(2,1)} async-done(((bf16[4,4,64,672]{3,2,1,0:T(8,128)(2,1)}), bf16[1,4,64,672]{3,2,1,0:T(8,128)(2,1)}) %reduce-scatter.3.cloned.1.call-update) | async-done | bytes 344080 | tf_op jit(solution)/shard_map/reduce_scatter | solution.py:110
  142.4 1.9 reshape.268
  145.7 16.8 %reduce-scatter.5.cloned.1.call-done = bf16[1,64,672]{2,1,0:T(8,128)(2,1)} async-done(((bf16[4,64,672]{2,1,0:T(8,128)(2,1)}), bf16[1,64,672]{2,1,0:T(8,128)(2,1)}) %reduce-scatter.5.cloned.1.call-update) | async-done | bytes 86032 | tf_op jit(solution)/shard_map/reduce_scatter | solution.py:113
  163.5 15.8 %all_gather.24 = bf16[4,64,672]{2,1,0:T(8,128)(2,1)} all-gather(bf16[1,64,672]{2,1,0:T(8,128)(2,1)S(1)} %multiply_convert_fusion.6), channel_id=1, replica_groups=mesh['groups'=2,'tile'=4,'segment'=2,'mp'=2] {'tile'}, dimensions={0}, use_global_device_ids=true | all-gather | bytes 430080 | tf_op jit(solution)/shard_map/all_gather | solution.py:128
  179.6 17.4 %all-gather.6.cloned.1.call-done = bf16[16,64,672]{2,1,0:T(8,128)(2,1)} async-done(((bf16[4,64,672]{2,1,0:T(8,128)(2,1)}), bf16[16,64,672]{2,1,0:T(8,128)(2,1)}) %all-gather.6.cloned.1.call-update) | async-done | bytes 1376272 | tf_op jit(solution)/shard_map/all_gather | solution.py:128
  197.0 2.7 convolution_convert_fusion.2
  199.8 9.2 %multiply_reduce_fusion = (f32[1024]{0:T(1024)S(1)}, bf16[1024,2048]{1,0:T(8,128)(2,1)S(1)}) fusion(f32[64,16,2048]{2,1,0:T(8,128)} %copy-done.1, f32[1024]{0:T(1024)S(1)} %rsqrt.37, bf16[1024,512]{1,0:T(8,128)(2,1)S(1)} %convolution_convert_fusion.2, bf16[4096,512]{1,0:T(8,128)(2,1)S(1)} %copy-done.13, s32[]{:T(128)S(6)} %select_n.50), kind=kOutput, calls=%fused_computation.1 | convolution fusion | flops 2191522816 | bytes 15736836 | tf_op jit(solution)/shard_map/dot_general | solution.py:49
  211.0 2.0 fusion.21
  216.2 86.1 %all-reduce.9.cloned.1.call-done = bf16[64,768]{1,0:T(8,128)(2,1)} async-done(((bf16[64,768]{1,0:T(8,128)(2,1)}), bf16[64,768]{1,0:T(8,128)(2,1)}) %all-reduce.9.cloned.1.call-update) | async-done | bytes 98320 | tf_op jit(solution)/shard_map/psum | solution.py:138
  304.0 3.1 convolution_convert_fusion.3
  313.6 17.2 %all-reduce.11.cloned.1.call-done = bf16[4,4,4,768]{3,2,0,1:T(4,128)(2,1)} async-done(((bf16[4,4,4,768]{3,2,0,1:T(4,128)(2,1)}), bf16[4,4,4,768]{3,2,0,1:T(4,128)(2,1)}) %all-reduce.11.cloned.1.call-update) | async-done | bytes 98320 | tf_op jit(solution)/shard_map/psum | solution.py:144
  333.1 13.3 %all-gather.3 = f32[4,224,16]{1,2,0:T(8,128)S(1)} all-gather(f32[1,224,16]{1,2,0:T(8,128)S(1)} %convolution_bitcast_fusion), channel_id=3, replica_groups=mesh['groups'=2,'tile'=4,'segment'=2,'mp'=2] {'tile'}, dimensions={0}, use_global_device_ids=true | all-gather | bytes 71680 | tf_op jit(solution)/shard_map/all_gather | solution.py:152
  (106 shorter events, 31.2 us)
Async XLA Ops:
  7.2 21.0 %copy-start = (bf16[1536,768]{1,0:T(8,128)(2,1)S(1)}, bf16[1536,768]{1,0:T(8,128)(2,1)}, u32[]{:S(2)}) copy-start(bf16[1536,768]{1,0:T(8,128)(2,1)} %param.14) | copy-start | bytes 7077892
  7.2 22.3 %copy-start.8 = (bf16[512,336]{0,1:T(8,128)(2,1)S(1)}, bf16[512,336]{0,1:T(8,128)(2,1)}, u32[]{:S(2)}) copy-start(bf16[512,336]{0,1:T(8,128)(2,1)} %param.19) | copy-start | bytes 1032196
  7.2 23.8 %copy-start.11 = (bf16[4,2048]{1,0:T(4,128)(2,1)S(1)}, bf16[4,2048]{1,0:T(4,128)(2,1)}, u32[]{:S(2)}) copy-start(bf16[4,2048]{1,0:T(4,128)(2,1)} %param.16) | copy-start | bytes 49156
  7.2 44.5 %all-reduce.5.cloned.1.call-start = ((), (), s32[]{:S(2)}) async-start(), calls=%async_computation.2 | async-start | bytes 196608 | tf_op jit(solution)/shard_map/psum | solution.py:93
  7.2 36.9 %copy-start.9 = (bf16[48,2048]{1,0:T(8,128)(2,1)S(1)}, bf16[48,2048]{1,0:T(8,128)(2,1)}, u32[]{:S(2)}) copy-start(bf16[48,2048]{1,0:T(8,128)(2,1)} %param.15) | copy-start | bytes 589828
  25.2 5.8 %copy-start.7 = (bf16[64,768]{1,0:T(8,128)(2,1)}, bf16[64,768]{1,0:T(8,128)(2,1)S(1)}, u32[]{:S(2)}) copy-start(bf16[64,768]{1,0:T(8,128)(2,1)S(1)} %multiply_convert_fusion.7) | copy-start | bytes 294916
  27.4 0.8 copy-start.3
  29.4 60.6 %all-reduce.7.cloned.1.call-start = ((), (), s32[]{:S(2)}) async-start(), calls=%async_computation.3 | async-start | bytes 524288 | tf_op jit(solution)/shard_map/psum | solution.py:87
  29.5 68.8 %collective-permute-start = (bf16[512,336]{0,1:T(8,128)(2,1)S(1)}, bf16[512,336]{0,1:T(8,128)(2,1)}, u32[]{:S(2)}, u32[]{:S(2)}) collective-permute-start(bf16[512,336]{0,1:T(8,128)(2,1)S(1)} %copy-done.8), channel_id=1, source_target_pairs={{0,1},{1,0},{2,3},{3,2},{4,5},{5,4},{6,7},{7,6},{8,9},{9,8},{10,11... | collective-permute-start | bytes 1032200 | tf_op jit(solution)/shard_map/ppermute | solution.py:15
  47.0 92.7 %reduce-scatter.3.cloned.1.call-start = ((), (), s32[]{:S(2)}) async-start(), calls=%async_computation.4 | async-start | bytes 1966080 | tf_op jit(solution)/shard_map/reduce_scatter | solution.py:110
  93.0 5.3 %copy-start.1 = (f32[64,16,2048]{2,1,0:T(8,128)}, f32[64,16,2048]{2,1,0:T(8,128)S(1)}, u32[]{:S(2)}) copy-start(f32[64,16,2048]{2,1,0:T(8,128)S(1)} %convolution_add_fusion) | copy-start | bytes 25165828
  100.9 0.9 copy-start.6
  109.0 31.0 %copy-start.12 = (s32[2,32]{1,0:T(2,128)S(1)}, s32[2,32]{1,0:T(2,128)}, u32[]{:S(2)}) copy-start(s32[2,32]{1,0:T(2,128)} %param.11) | copy-start | bytes 772
  109.0 31.4 %copy-start.2 = (bf16[2,8,48,224]{3,2,1,0:T(8,128)(2,1)S(1)}, bf16[2,8,48,224]{3,2,1,0:T(8,128)(2,1)}, u32[]{:S(2)}) copy-start(bf16[2,8,48,224]{3,2,1,0:T(8,128)(2,1)} %param.10) | copy-start | bytes 1032196
  111.6 50.9 %reduce-scatter.5.cloned.1.call-start = ((), (), s32[]{:S(2)}) async-start(), calls=%async_computation.5 | async-start | bytes 491520 | tf_op jit(solution)/shard_map/reduce_scatter | solution.py:113
  139.8 57.2 %all-gather.6.cloned.1.call-start = ((), (), s32[]{:S(2)}) async-start(), calls=%async_computation.8 | async-start | bytes 1966080 | tf_op jit(solution)/shard_map/all_gather | solution.py:128
  179.3 122.9 %all-reduce.9.cloned.1.call-start = ((), (), s32[]{:S(2)}) async-start(), calls=%async_computation.6 | async-start | bytes 196608 | tf_op jit(solution)/shard_map/psum | solution.py:138
  197.0 2.9 copy-start.13
  199.8 9.2 %copy-start.10 = (bf16[48,2048]{1,0:T(8,128)(2,1)S(1)}, bf16[48,2048]{1,0:T(8,128)(2,1)}, u32[]{:S(2)}) copy-start(bf16[48,2048]{1,0:T(8,128)(2,1)} %param.15) | copy-start | bytes 589828
  199.8 9.7 %copy-start.14 = (bf16[64,16,2048]{2,1,0:T(8,128)(2,1)S(1)}, bf16[64,16,2048]{2,1,0:T(8,128)(2,1)}, u32[]{:S(2)}) copy-start(bf16[64,16,2048]{2,1,0:T(8,128)(2,1)} %get-tuple-element.6) | copy-start | bytes 12582916
  209.5 1.5 copy-start.5
  211.0 91.3 %copy-start.4 = (f32[64,1536]{1,0:T(8,128)S(1)}, f32[64,1536]{1,0:T(8,128)}, u32[]{:S(2)}) copy-start(f32[64,1536]{1,0:T(8,128)} %copy-done.3) | copy-start | bytes 1179652
  215.0 115.8 %all-reduce.11.cloned.1.call-start = ((), (), s32[]{:S(2)}) async-start(), calls=%async_computation.7 | async-start | bytes 196608 | tf_op jit(solution)/shard_map/psum | solution.py:144
Sparse Core Ops, SparseCore 0:
  29.5 22.1 all-reduce.4
  54.6 35.3 all-reduce.6
  111.8 27.9 reduce-scatter.2
  141.9 20.5 reduce-scatter.4
  179.5 17.4 all-gather.5
  215.1 87.0 all-reduce.8
  310.8 20.0 all-reduce.10
